TPU v7x, 32 devices: a whole 2x2x4 slice. The times are simulated.
32 devices in a mesh: dp: 8 (over z, y), head: 4 (over x, core).
Axes of the slice: x: 2, y: 2, z: 4, core: 2. Of those that a mesh axis runs over, the one named last changes fastest.
Arguments:
- segment: bfloat16 [8, 512, 1024], P('dp'), may hold values from -6 to 6
- memory: bfloat16 [8, 512, 1024], P('dp'), may hold values from -6 to 6
- compressed: bfloat16 [8, 512, 1024], P('dp'), may hold values from -6 to 6
- mem_fill: int32 [8], P('dp'), may hold values from 0 to 512, as said below
- comp_fill: int32 [8], P('dp'), may hold values from 0 to 512, as said below
- gain_attn: float32 [1024], replicated, may hold values from 0.1 to 1.9
- w_qkv: bfloat16 [1024, 3072], P(None, 'head'), may hold values from -0.1875 to 0.1875
- content_bias: float32 [128, 8], P(None, 'head'), may hold values from -3 to 3
- position_bias: float32 [128, 8], P(None, 'head'), may hold values from -3 to 3
- w_rel: bfloat16 [1024, 1024], P(None, 'head'), may hold values from -0.1875 to 0.1875
- w_out: bfloat16 [1024, 1024], P(None, 'head'), may hold values from -1 to 1
- gain_ffn: float32 [1024], replicated, may hold values from 0.1 to 1.9
- w_up: bfloat16 [1024, 4096], P(None, 'head'), may hold values from -0.1875 to 0.1875
- w_down: bfloat16 [1024, 4096], P(None, 'head'), may hold values from -0.09375 to 0.09375
- w_comp: bfloat16 [3072, 1024], P(None, 'head'), may hold values from -0.109375 to 0.109375
- out_cotangent: bfloat16 [8, 512, 1024], P('dp'), may hold values from -6 to 6
- comp_cotangent: bfloat16 [8, 170, 1024], P('dp', None, 'head'), may hold values from -6 to 6
Outputs:
- layer_output: bfloat16 [8, 512, 1024], P('dp')
- new_compressed: bfloat16 [8, 170, 1024], P('dp', None, 'head')
- input_grad: float32 [8, 512, 1024], P('dp')
- gain_attn_grad: float32 [1024], P('dp')
- qkv_grad: float32 [1024, 3072], P('dp', 'head')
- content_bias_grad: float32 [128, 8], P('dp', 'head')
- position_bias_grad: float32 [128, 8], P('dp', 'head')
- rel_grad: float32 [1024, 1024], P('dp', 'head')
- out_proj_grad: float32 [1024, 1024], P('dp', 'head')
- gain_ffn_grad: float32 [1024], P('dp')
- up_grad: float32 [1024, 4096], P('dp', 'head')
- down_grad: float32 [1024, 4096], P('dp', 'head')
- comp_grad: float32 [3072, 1024], P('dp', 'head')
Inputs may be any that keep to these rules, and one draw needn't show every extreme that they name: `mem_fill`: the empty memory slots of a stream are its oldest ones; streams whose memory is empty are common. `comp_fill`: the empty compressed slots are the oldest ones; a stream has compressed rows only where its memory is full.
All inputs are finite; a program needn't handle non-finite values.
Results may differ from a plain program's by a relative error of at most 0.017.
Values sent between devices are 32-bit elements; how exact they have to be, the bound alone decides.
A program may use at most 192 MiB of HBM per device.

v0:
```python
import jax
import jax.numpy as jnp
from jax import lax
from jax.sharding import PartitionSpec as P

epsilon = 1e-05
masked_value = -1e30


def norm_rows(rows, gain):
    average = jnp.mean(rows, axis=-1, keepdims=True)
    centered = rows - average
    spread = jnp.mean(centered * centered, axis=-1, keepdims=True)
    return centered * lax.rsqrt(spread + epsilon) * gain


def angle_tables(model_width, row_count):
    half_width = model_width // 2
    frequency = jnp.exp(-jnp.log(10000.0) * jnp.arange(half_width, dtype=jnp.float32) / half_width)
    angles = jnp.arange(row_count, dtype=jnp.float32)[:, None] * frequency[None, :]
    return (jnp.sin(angles), jnp.cos(angles))


def rotate_rows(values, sine_rows, cosine_rows):
    half_width = values.shape[-1] // 2
    sine_rows = sine_rows[:, None, :]
    cosine_rows = cosine_rows[:, None, :]
    leading = values[..., :half_width]
    trailing = values[..., half_width:]
    return jnp.concatenate(
        [
            leading * sine_rows + trailing * cosine_rows,
            trailing * sine_rows - leading * cosine_rows,
        ],
        axis=-1,
    )


def unrotate_rows(grads, sine_rows, cosine_rows):
    half_width = grads.shape[-1] // 2
    sine_rows = sine_rows[:, None, :]
    cosine_rows = cosine_rows[:, None, :]
    upper_grad = grads[..., :half_width]
    lower_grad = grads[..., half_width:]
    return jnp.concatenate(
        [
            upper_grad * sine_rows - lower_grad * cosine_rows,
            upper_grad * cosine_rows + lower_grad * sine_rows,
        ],
        axis=-1,
    )


def shards(
    segment,
    memory,
    compressed,
    mem_fill,
    comp_fill,
    gain_attn,
    w_qkv,
    content_bias,
    position_bias,
    w_rel,
    w_out,
    gain_ffn,
    w_up,
    w_down,
    w_comp,
    out_cotangent,
    comp_cotangent,
):
    model_width = segment.shape[2]
    seg_rows = segment.shape[1]
    mem_rows = memory.shape[1]
    comp_rows = compressed.shape[1]
    prior_rows = comp_rows + mem_rows
    key_count = prior_rows + seg_rows
    head_size = content_bias.shape[0]
    heads_here = content_bias.shape[1]
    inner_width = heads_here * head_size
    new_count = comp_cotangent.shape[1]
    score_scale = head_size ** (-0.5)
    qkv_split = w_qkv.reshape(model_width, heads_here, 3, head_size)
    w_query = qkv_split[:, :, 0].reshape(model_width, inner_width)
    w_keyval = qkv_split[:, :, 1:].reshape(model_width, 2 * inner_width)
    rel_split = w_rel.reshape(model_width, heads_here, head_size)
    sine_table, cosine_table = angle_tables(model_width, key_count)
    query_sine = sine_table[prior_rows:]
    query_cosine = cosine_table[prior_rows:]
    key_features = jnp.concatenate([cosine_table, sine_table], axis=-1).astype(jnp.bfloat16)
    bounds = ((0, comp_rows), (comp_rows, prior_rows), (prior_rows, key_count))
    query_index = jnp.arange(seg_rows)[:, None]

    def block_valid(block_index, fill_count):
        start_key, end_key = bounds[block_index]
        key_index = jnp.arange(start_key, end_key)[None, :]
        if fill_count is None:
            return key_index - start_key <= query_index
        return jnp.broadcast_to(key_index >= end_key - fill_count, (seg_rows, end_key - start_key))

    def block_scores(block_index, fill_count, content_q, rotated, key_rows):
        start_key, end_key = bounds[block_index]
        content = jnp.einsum(
            "shc,khc->hsk",
            content_q,
            key_rows[start_key:end_key],
            preferred_element_type=jnp.float32,
        )
        place = jnp.einsum(
            "shd,kd->hsk",
            rotated,
            key_features[start_key:end_key],
            preferred_element_type=jnp.float32,
        )
        scores = (content + place) * score_scale
        return jnp.where(block_valid(block_index, fill_count)[None], scores, masked_value)

    def forward_stream(seg_low, mem_low, comp_low, fills):
        all_rows = jnp.concatenate([comp_low, mem_low, seg_low], axis=0).astype(jnp.float32)
        normed = norm_rows(all_rows, gain_attn).astype(jnp.bfloat16)
        queries = jnp.dot(normed[prior_rows:], w_query, preferred_element_type=jnp.float32).reshape(
            seg_rows, heads_here, head_size
        )
        keyval = jnp.dot(normed, w_keyval, preferred_element_type=jnp.float32).reshape(
            key_count, heads_here, 2, head_size
        )
        key_rows = keyval[:, :, 0].astype(jnp.bfloat16)
        value_rows = keyval[:, :, 1].astype(jnp.bfloat16)
        content_q = (queries + content_bias.T[None]).astype(jnp.bfloat16)
        pos_in = (queries + position_bias.T[None]).astype(jnp.bfloat16)
        rel_proj = jnp.einsum("shc,dhc->shd", pos_in, rel_split, preferred_element_type=jnp.float32)
        rotated = rotate_rows(rel_proj, query_sine, query_cosine).astype(jnp.bfloat16)
        masked = [
            block_scores(block_index, fills[block_index], content_q, rotated, key_rows)
            for block_index in range(3)
        ]
        row_top = jnp.max(masked[0], axis=-1, keepdims=True)
        row_top = jnp.maximum(row_top, jnp.max(masked[1], axis=-1, keepdims=True))
        row_top = jnp.maximum(row_top, jnp.max(masked[2], axis=-1, keepdims=True))
        raised = [jnp.exp(block - row_top) for block in masked]
        row_total = (
            jnp.sum(raised[0], axis=-1, keepdims=True)
            + jnp.sum(raised[1], axis=-1, keepdims=True)
            + jnp.sum(raised[2], axis=-1, keepdims=True)
        )
        mixed = jnp.zeros((seg_rows, heads_here, head_size), jnp.float32)
        for block_index in range(3):
            start_key, end_key = bounds[block_index]
            probs_low = (raised[block_index] / row_total).astype(jnp.bfloat16)
            mixed = mixed + jnp.einsum(
                "hsk,khc->shc",
                probs_low,
                value_rows[start_key:end_key],
                preferred_element_type=jnp.float32,
            )
        mixed = mixed.astype(jnp.bfloat16).reshape(seg_rows, inner_width)
        log_total = row_top + jnp.log(row_total)
        return (normed, content_q, pos_in, rotated, key_rows, value_rows, mixed, log_total)

    def forward_step(totals, stream):
        seg_low, mem_low, comp_low, mem_count, comp_count, out_grad, new_grad = stream
        fills = (comp_count, mem_count, None)
        saved = forward_stream(seg_low, mem_low, comp_low, fills)
        mixed = saved[6]
        attn_part = jnp.einsum("sc,dc->sd", mixed, w_out, preferred_element_type=jnp.float32)
        attention = lax.psum(attn_part, "head")
        residual = seg_low.astype(jnp.float32) + attention
        normed_ffn, ffn_pull = jax.vjp(norm_rows, residual, gain_ffn)
        normed_low = normed_ffn.astype(jnp.bfloat16)
        hidden = jnp.dot(normed_low, w_up, preferred_element_type=jnp.float32)
        activated_full, gelu_pull = jax.vjp(jax.nn.gelu, hidden)
        activated = activated_full.astype(jnp.bfloat16)
        ffn_part = jnp.einsum("sf,df->sd", activated, w_down, preferred_element_type=jnp.float32)
        ffn_out = lax.psum(ffn_part, "head")
        layer_output = (residual + ffn_out).astype(jnp.bfloat16)
        memory_valid = (jnp.arange(mem_rows) >= mem_rows - mem_count).astype(jnp.bfloat16)
        windows = (mem_low * memory_valid[:, None])[: 3 * new_count].reshape(
            new_count, 3 * model_width
        )
        new_rows = jnp.dot(windows, w_comp, preferred_element_type=jnp.float32).astype(jnp.bfloat16)
        down_part = jnp.einsum("sd,sf->df", out_grad, activated, preferred_element_type=jnp.float32)
        act_grad = jnp.einsum("sd,df->sf", out_grad, w_down, preferred_element_type=jnp.float32)
        hidden_grad = gelu_pull(act_grad)[0].astype(jnp.bfloat16)
        up_part = jnp.einsum(
            "sd,sf->df", normed_low, hidden_grad, preferred_element_type=jnp.float32
        )
        ffn_normed_part = jnp.einsum(
            "sf,df->sd", hidden_grad, w_up, preferred_element_type=jnp.float32
        )
        ffn_normed_grad = lax.psum(ffn_normed_part, "head")
        res_part, gain_part = ffn_pull(ffn_normed_grad)
        residual_grad = out_grad.astype(jnp.float32) + res_part
        comp_part = jnp.einsum("rk,rd->kd", windows, new_grad, preferred_element_type=jnp.float32)
        totals = (
            totals[0] + up_part,
            totals[1] + down_part,
            totals[2] + gain_part,
            totals[3] + comp_part,
        )
        return (totals, (layer_output, new_rows, residual_grad) + saved)

    def backward_step(totals, stream):
        (
            seg_low,
            mem_low,
            comp_low,
            mem_count,
            comp_count,
            residual_grad,
            normed,
            content_q,
            pos_in,
            rotated,
            key_rows,
            value_rows,
            mixed,
            log_total,
        ) = stream
        fills = (comp_count, mem_count, None)
        attn_grad = residual_grad.astype(jnp.bfloat16)
        out_part = jnp.einsum("sd,sc->dc", attn_grad, mixed, preferred_element_type=jnp.float32)
        mixed_grad = (
            jnp.einsum("sd,dc->sc", attn_grad, w_out, preferred_element_type=jnp.float32)
            .astype(jnp.bfloat16)
            .reshape(seg_rows, heads_here, head_size)
        )
        probs_list = []
        prob_grads = []
        row_delta = jnp.zeros((heads_here, seg_rows, 1), jnp.float32)
        for block_index in range(3):
            start_key, end_key = bounds[block_index]
            masked = block_scores(block_index, fills[block_index], content_q, rotated, key_rows)
            probs = jnp.exp(masked - log_total)
            prob_grad = jnp.einsum(
                "shc,khc->hsk",
                mixed_grad,
                value_rows[start_key:end_key],
                preferred_element_type=jnp.float32,
            )
            row_delta = row_delta + jnp.sum(probs * prob_grad, axis=-1, keepdims=True)
            probs_list.append(probs)
            prob_grads.append(prob_grad)
        content_sum = jnp.zeros((seg_rows, heads_here, head_size), jnp.float32)
        rotated_sum = jnp.zeros((seg_rows, heads_here, model_width), jnp.float32)
        key_parts = []
        value_parts = []
        for block_index in range(3):
            start_key, end_key = bounds[block_index]
            score_grad = (probs_list[block_index] * (prob_grads[block_index] - row_delta)).astype(
                jnp.bfloat16
            )
            probs_low = probs_list[block_index].astype(jnp.bfloat16)
            content_sum = content_sum + jnp.einsum(
                "hsk,khc->shc",
                score_grad,
                key_rows[start_key:end_key],
                preferred_element_type=jnp.float32,
            )
            rotated_sum = rotated_sum + jnp.einsum(
                "hsk,kd->shd",
                score_grad,
                key_features[start_key:end_key],
                preferred_element_type=jnp.float32,
            )
            key_parts.append(
                jnp.einsum(
                    "hsk,shc->khc", score_grad, content_q, preferred_element_type=jnp.float32
                )
            )
            value_parts.append(
                jnp.einsum(
                    "hsk,shc->khc", probs_low, mixed_grad, preferred_element_type=jnp.float32
                )
            )
        content_grad = content_sum * score_scale
        rotated_grad = rotated_sum * score_scale
        key_grad = jnp.concatenate(key_parts, axis=0) * score_scale
        value_grad = jnp.concatenate(value_parts, axis=0)
        rel_low = unrotate_rows(rotated_grad, query_sine, query_cosine).astype(jnp.bfloat16)
        rel_part = jnp.einsum(
            "shd,shc->dhc", rel_low, pos_in, preferred_element_type=jnp.float32
        ).reshape(model_width, inner_width)
        pos_grad = jnp.einsum(
            "shd,dhc->shc", rel_low, rel_split, preferred_element_type=jnp.float32
        )
        content_bias_part = jnp.sum(content_grad, axis=0).T
        position_bias_part = jnp.sum(pos_grad, axis=0).T
        query_low = (content_grad + pos_grad).astype(jnp.bfloat16).reshape(seg_rows, inner_width)
        keyval_low = (
            jnp.stack([key_grad, value_grad], axis=2)
            .astype(jnp.bfloat16)
            .reshape(key_count, 2 * inner_width)
        )
        query_part = jnp.einsum(
            "sd,sc->dc", normed[prior_rows:], query_low, preferred_element_type=jnp.float32
        ).reshape(model_width, heads_here, 1, head_size)
        keyval_part = jnp.einsum(
            "kd,kc->dc", normed, keyval_low, preferred_element_type=jnp.float32
        ).reshape(model_width, heads_here, 2, head_size)
        qkv_part = jnp.concatenate([query_part, keyval_part], axis=2).reshape(
            model_width, 3 * inner_width
        )
        normed_grad = jnp.einsum(
            "kc,dc->kd", keyval_low, w_keyval, preferred_element_type=jnp.float32
        )
        seg_normed_part = normed_grad[prior_rows:] + jnp.einsum(
            "sc,dc->sd", query_low, w_query, preferred_element_type=jnp.float32
        )
        prior_all = jnp.concatenate([comp_low, mem_low], axis=0).astype(jnp.float32)
        prior_hat = norm_rows(prior_all, jnp.ones((model_width,), jnp.float32))
        prior_gain = jnp.sum(normed_grad[:prior_rows] * prior_hat, axis=0)
        seg_normed_grad, prior_gain_sum = lax.psum((seg_normed_part, prior_gain), "head")
        seg_normed, norm_pull = jax.vjp(norm_rows, seg_low.astype(jnp.float32), gain_attn)
        seg_grad, seg_gain = norm_pull(seg_normed_grad)
        input_grad = residual_grad + seg_grad
        totals = (
            totals[0] + qkv_part,
            totals[1] + content_bias_part,
            totals[2] + position_bias_part,
            totals[3] + rel_part,
            totals[4] + out_part,
            totals[5] + seg_gain + prior_gain_sum,
        )
        return (totals, input_grad)

    ffn_zero = (
        jnp.zeros(w_up.shape, jnp.float32),
        jnp.zeros(w_down.shape, jnp.float32),
        jnp.zeros(gain_ffn.shape, jnp.float32),
        jnp.zeros(w_comp.shape, jnp.float32),
    )
    ffn_totals, kept = lax.scan(
        forward_step,
        ffn_zero,
        (segment, memory, compressed, mem_fill, comp_fill, out_cotangent, comp_cotangent),
    )
    attn_zero = (
        jnp.zeros(w_qkv.shape, jnp.float32),
        jnp.zeros(content_bias.shape, jnp.float32),
        jnp.zeros(position_bias.shape, jnp.float32),
        jnp.zeros(w_rel.shape, jnp.float32),
        jnp.zeros(w_out.shape, jnp.float32),
        jnp.zeros(gain_attn.shape, jnp.float32),
    )
    attn_totals, input_grad = lax.scan(
        backward_step,
        attn_zero,
        (segment, memory, compressed, mem_fill, comp_fill) + tuple(kept[2:]),
    )
    (
        qkv_sum,
        cbias_sum,
        pbias_sum,
        rel_sum,
        out_sum,
        gain_attn_sum,
        up_sum,
        down_sum,
        gain_ffn_sum,
        comp_sum,
    ) = (
        lax.psum_scatter(attn_totals[0], "dp", scatter_dimension=0, tiled=True),
        lax.psum_scatter(attn_totals[1], "dp", scatter_dimension=0, tiled=True),
        lax.psum_scatter(attn_totals[2], "dp", scatter_dimension=0, tiled=True),
        lax.psum_scatter(attn_totals[3], "dp", scatter_dimension=0, tiled=True),
        lax.psum_scatter(attn_totals[4], "dp", scatter_dimension=0, tiled=True),
        lax.psum_scatter(attn_totals[5], "dp", scatter_dimension=0, tiled=True),
        lax.psum_scatter(ffn_totals[0], "dp", scatter_dimension=0, tiled=True),
        lax.psum_scatter(ffn_totals[1], "dp", scatter_dimension=0, tiled=True),
        lax.psum_scatter(ffn_totals[2], "dp", scatter_dimension=0, tiled=True),
        lax.psum_scatter(ffn_totals[3], "dp", scatter_dimension=0, tiled=True),
    )
    return (
        kept[0],
        kept[1],
        input_grad,
        gain_attn_sum,
        qkv_sum,
        cbias_sum,
        pbias_sum,
        rel_sum,
        out_sum,
        gain_ffn_sum,
        up_sum,
        down_sum,
        comp_sum,
    )


def solution(mesh):
    placed = (
        P("dp", None, None),
        P("dp", None, None),
        P("dp", None, None),
        P("dp"),
        P("dp"),
        P(),
        P(None, "head"),
        P(None, "head"),
        P(None, "head"),
        P(None, "head"),
        P(None, "head"),
        P(),
        P(None, "head"),
        P(None, "head"),
        P(None, "head"),
        P("dp", None, None),
        P("dp", None, "head"),
    )
    return jax.shard_map(
        shards,
        mesh=mesh,
        in_specs=placed,
        out_specs=(
            P("dp", None, None),
            P("dp", None, "head"),
            P("dp", None, None),
            P("dp"),
            P("dp", "head"),
            P("dp", "head"),
            P("dp", "head"),
            P("dp", "head"),
            P("dp", "head"),
            P("dp"),
            P("dp", "head"),
            P("dp", "head"),
            P("dp", "head"),
        ),
        check_vma=False,
    )
```

profile of v0, /device:TPU:0, one launch (start us, length us, event | category | flops | bytes accessed | tf_op | source)
XLA Modules:
  0.0 895.2 jit_solution(563253083210776698)
XLA Ops:
  8.1 2.4 convert_reduce_fusion
  10.5 3.0 fusion.2
  13.6 2.6 copy.116
  16.2 3.9 fusion.4
  32.0 12.2 %fusion.57 = (bf16[1536,512]{1,0:T(8,128)(2,1)S(1)}, bf16[1536,512]{1,0:T(8,128)(2,1)S(1)}, f32[1536,512]{1,0:T(8,128)S(1)}, f32[1536,512]{1,0:T(8,128)S(1)}) fusion(f32[512]{0:T(512)S(1)} %multiply_exponential_fusion), kind=kLoop, calls=%fused_computation.126 | loop fusion | flops 2359296 | bytes 9439232 | tf_op jit(solution)/shard_map/convert.5
  60.4 54.0 %all-reduce.8.cloned.1.call-done = f32[512,1024]{1,0:T(8,128)} async-done(((f32[512,1024]{1,0:T(8,128)}), f32[512,1024]{1,0:T(8,128)}) %all-reduce.8.cloned.1.call-update) | async-done | bytes 2097168 | tf_op jit(solution)/shard_map/while/body/eval_jaxpr/psum | solution.py:167
  122.7 2.6 fusion.122
  127.3 5.1 fusion.111
  132.4 44.5 %all-reduce.10.cloned.1.call-done = f32[512,1024]{1,0:T(8,128)} async-done(((f32[512,1024]{1,0:T(8,128)}), f32[512,1024]{1,0:T(8,128)}) %all-reduce.10.cloned.1.call-update) | async-done | bytes 2097168 | tf_op jit(solution)/shard_map/while/body/eval_jaxpr/psum | solution.py:191
  177.0 2.4 multiply_reduce_fusion
  206.0 4.5 convolution_bitcast_fusion
  211.3 3.6 slice_add_fusion
  215.2 5.4 convolution_bitcast_fusion.1
  220.6 2.7 fusion.123
  223.4 3.2 fusion.49
  226.6 2.6 copy.159
  232.8 3.5 fusion.96
  238.2 3.7 fusion.10
  244.0 3.5 copy.157
  247.6 4.8 fusion.113
  257.1 3.3 fusion.9
  260.4 5.8 psum.44
  267.6 60.3 %reduce-scatter.27.cloned.1.call-done = f32[16,2]{1,0:T(8,128)} async-done(((f32[128,2]{1,0:T(8,128)}), f32[16,2]{1,0:T(8,128)}) %reduce-scatter.27.cloned.1.call-update) | async-done | bytes 144
  329.2 85.7 %all-reduce.12.cloned.1.call-done = (f32[512,1024]{1,0:T(8,128)}, f32[512,1024]{1,0:T(8,128)}) async-done(((f32[512,1024]{1,0:T(8,128)}, f32[512,1024]{1,0:T(8,128)}), (f32[512,1024]{1,0:T(8,128)}, f32[512,1024]{1,0:T(8,128)})) %all-reduce.12.cloned.1.call-update) | async-done | bytes 4194320 | tf_op jit(solution)/shard_map/while/body/eval_jaxpr/psum | solution.py:175
  418.4 22.5 %all-reduce.2 = (f32[1024]{0:T(1024)S(1)}, f32[1024]{0:T(1024)S(1)}) all-reduce(f32[1024]{0:T(1024)S(1)} %add.318, f32[1024]{0:T(1024)S(1)} %get-tuple-element.228), channel_id=2, replica_groups=mesh['dp'=8,'head'=4] {'dp'}, use_global_device_ids=true, to_apply=%region_28.29.clone | all-reduce | flops 2048 | bytes 16384
  442.1 5.8 add_bitcast_fusion
  447.9 59.7 %reduce-scatter.21.cloned.1.call-done = f32[128,1024]{0,1:T(8,128)} async-done(((f32[1024,1024]{0,1:T(8,128)}), f32[128,1024]{0,1:T(8,128)}) %reduce-scatter.21.cloned.1.call-update) | async-done | bytes 524304 | tf_op jit(solution)/shard_map/reduce_scatter | solution.py:370
  509.6 65.2 %reduce-scatter.17.cloned.1.call-done = f32[128,256]{1,0:T(8,128)} async-done(((f32[1024,256]{1,0:T(8,128)}), f32[128,256]{1,0:T(8,128)}) %reduce-scatter.17.cloned.1.call-update) | async-done | bytes 131088 | tf_op jit(solution)/shard_map/reduce_scatter | solution.py:367
  574.8 66.9 %reduce-scatter.15.cloned.1.call-done = f32[128,256]{1,0:T(8,128)} async-done(((f32[1024,256]{1,0:T(8,128)}), f32[128,256]{1,0:T(8,128)}) %reduce-scatter.15.cloned.1.call-update) | async-done | bytes 131088 | tf_op jit(solution)/shard_map/reduce_scatter | solution.py:366
  641.7 77.6 %reduce-scatter.23.cloned.1.call-done = f32[384,256]{1,0:T(8,128)} async-done(((f32[3072,256]{1,0:T(8,128)}), f32[384,256]{1,0:T(8,128)}) %reduce-scatter.23.cloned.1.call-update) | async-done | bytes 393232 | tf_op jit(solution)/shard_map/reduce_scatter | solution.py:372
  719.3 77.6 %reduce-scatter.13.cloned.1.call-done = f32[128,768]{1,0:T(8,128)} async-done(((f32[1024,768]{1,0:T(8,128)}), f32[128,768]{1,0:T(8,128)}) %reduce-scatter.13.cloned.1.call-update) | async-done | bytes 393232 | tf_op jit(solution)/shard_map/reduce_scatter | solution.py:363
  796.9 91.3 %reduce-scatter.19.cloned.1.call-done = f32[128,1024]{1,0:T(8,128)} async-done(((f32[1024,1024]{1,0:T(8,128)}), f32[128,1024]{1,0:T(8,128)}) %reduce-scatter.19.cloned.1.call-update) | async-done | bytes 524304 | tf_op jit(solution)/shard_map/reduce_scatter | solution.py:369
  (232 shorter events, 86.0 us)
Async XLA Ops:
  7.2 109.9 %copy-start = (bf16[1024,1024]{1,0:T(8,128)(2,1)S(1)}, bf16[1024,1024]{1,0:T(8,128)(2,1)}, u32[]{:S(2)}) copy-start(bf16[1024,1024]{1,0:T(8,128)(2,1)} %param.29) | copy-start | bytes 6291460
  7.2 3.3 copy-start.4
  7.2 107.2 %all-reduce.8.cloned.1.call-start = ((), (), s32[]{:S(2)}) async-start(), calls=%async_computation.8 | async-start | bytes 4194304 | tf_op jit(solution)/shard_map/while/body/eval_jaxpr/psum | solution.py:167
  7.3 3.3 copy-start.5
  7.3 3.3 copy-start.8
  13.5 2.6 copy-start.57
  16.2 3.9 copy-start.35
  22.0 4.8 copy-start.32
  44.2 7.3 copy-start.16
  44.2 7.3 copy-start.18
  50.1 7.0 copy-start.10
  52.4 4.1 copy-start.12
  60.1 116.8 %all-reduce.10.cloned.1.call-start = ((), (), s32[]{:S(2)}) async-start(), calls=%async_computation.9 | async-start | bytes 4194304 | tf_op jit(solution)/shard_map/while/body/eval_jaxpr/psum | solution.py:191
  125.3 140.9 %reduce-scatter.25.cloned.1.call-start = ((), (), s32[]{:S(2)}) async-start(), calls=%async_computation.16 | async-start | bytes 73728
  127.3 49.7 %copy-start.3 = (f32[512,1024]{1,0:T(8,128)S(1)}, f32[512,1024]{1,0:T(8,128)}, u32[]{:S(2)}) copy-start(f32[512,1024]{1,0:T(8,128)} %copy-done.2) | copy-start | bytes 6291460
  182.6 2.6 copy-start.15
  191.1 2.6 copy-start.17
  202.8 125.1 %reduce-scatter.27.cloned.1.call-start = ((), (), s32[]{:S(2)}) async-start(), calls=%async_computation.17 | async-start | bytes 73728
  202.9 3.1 copy-start.36
  204.2 6.3 copy-start.49
  206.0 4.5 copy-start.51
  211.2 203.7 %all-reduce.12.cloned.1.call-start = ((), (), s32[]{:S(2)}) async-start(), calls=%async_computation.18 | async-start | bytes 8388608 | tf_op jit(solution)/shard_map/while/body/eval_jaxpr/psum | solution.py:175
  214.9 292.7 %reduce-scatter.21.cloned.1.call-start = ((), (), s32[]{:S(2)}) async-start(), calls=%async_computation.14 | async-start | bytes 4718592 | tf_op jit(solution)/shard_map/reduce_scatter | solution.py:370
  220.6 354.3 %reduce-scatter.17.cloned.1.call-start = ((), (), s32[]{:S(2)}) async-start(), calls=%async_computation.12 | async-start | bytes 1179648 | tf_op jit(solution)/shard_map/reduce_scatter | solution.py:367
  223.4 418.4 %reduce-scatter.15.cloned.1.call-start = ((), (), s32[]{:S(2)}) async-start(), calls=%async_computation.11 | async-start | bytes 1179648 | tf_op jit(solution)/shard_map/reduce_scatter | solution.py:366
  229.2 490.2 %reduce-scatter.23.cloned.1.call-start = ((), (), s32[]{:S(2)}) async-start(), calls=%async_computation.15 | async-start | bytes 3538944 | tf_op jit(solution)/shard_map/reduce_scatter | solution.py:372
  229.3 3.5 copy-start.56
  236.3 560.6 %reduce-scatter.13.cloned.1.call-start = ((), (), s32[]{:S(2)}) async-start(), calls=%async_computation.10 | async-start | bytes 3538944 | tf_op jit(solution)/shard_map/reduce_scatter | solution.py:363
  247.5 640.7 %reduce-scatter.19.cloned.1.call-start = ((), (), s32[]{:S(2)}) async-start(), calls=%async_computation.13 | async-start | bytes 4718592 | tf_op jit(solution)/shard_map/reduce_scatter | solution.py:369
  257.1 157.8 %copy-start.6 = (bf16[1,512,1024]{2,1,0:T(8,128)(2,1)S(1)}, bf16[1,512,1024]{2,1,0:T(8,128)(2,1)}, u32[]{:S(2)}) copy-start(bf16[1,512,1024]{2,1,0:T(8,128)(2,1)} %param.17) | copy-start | bytes 3145732
  417.3 24.7 %copy-start.7 = (bf16[1,512,1024]{2,1,0:T(8,128)(2,1)S(1)}, bf16[1,512,1024]{2,1,0:T(8,128)(2,1)}, u32[]{:S(2)}) copy-start(bf16[1,512,1024]{2,1,0:T(8,128)(2,1)} %param.17) | copy-start | bytes 3145732
  442.1 446.2 %copy-start.1 = (bf16[1024,1024]{1,0:T(8,128)(2,1)S(1)}, bf16[1024,1024]{1,0:T(8,128)(2,1)}, u32[]{:S(2)}) copy-start(bf16[1024,1024]{1,0:T(8,128)(2,1)} %param.29) | copy-start | bytes 6291460
  (42 other events, 71.8 us)
Sparse Core Ops, SparseCore 0:
  60.3 54.0 all-reduce.7
  125.5 51.4 all-reduce.9
  203.0 61.3 reduce-scatter.24
  267.6 60.2 reduce-scatter.26
  330.2 84.6 all-reduce.11
  418.8 88.6 reduce-scatter.20
  511.5 63.2 reduce-scatter.16
  579.2 62.5 reduce-scatter.14
  645.9 73.3 reduce-scatter.22
  723.3 73.5 reduce-scatter.12
  801.1 87.0 reduce-scatter.18
where the time goes:
time: 902 us; the launch traced here: 895 us
  waiting for transfers between devices  683 us (76%)
  matrix products  78.6 us (9%)
  other arithmetic  53 us (6%)
  local copies, waits for them, and re-layouts  34.2 us (4%)
  blocking collectives  28.3 us (3%)
  between operations  17.2 us (2%)
    reduce_scatter x1, waiting for transfers between devices, shards(): lax.psum_scatter(ffn_totals[0], 'dp', scatter_dimension=0, tiled=True)  91.3 us
    psum x1, waiting for transfers between devices, forward_step(): ffn_out = lax.psum(ffn_part, 'head')  85.7 us
    reduce_scatter x1, waiting for transfers between devices, shards(): lax.psum_scatter(ffn_totals[3], 'dp', scatter_dimension=0, tiled=True)  77.6 us
    reduce_scatter x1, waiting for transfers between devices, shards(): lax.psum_scatter(attn_totals[0], 'dp', scatter_dimension=0, tiled=True)  77.6 us
    reduce_scatter x1, waiting for transfers between devices, shards(): lax.psum_scatter(attn_totals[3], 'dp', scatter_dimension=0, tiled=True)  66.9 us
    reduce_scatter x1, waiting for transfers between devices, shards(): lax.psum_scatter(attn_totals[4], 'dp', scatter_dimension=0, tiled=True)  65.2 us
    unnamed x13, waiting for transfers between devices  60.5 us
    reduce_scatter x1, waiting for transfers between devices, shards(): lax.psum_scatter(ffn_totals[1], 'dp', scatter_dimension=0, tiled=True)  59.7 us
  transfers between devices with their start and end apart: 11, of which 10 were waited for; matrix products, arithmetic and copies ran while one was open for 9% of the time, Pallas kernels for 0%

commit v1 on v0

v1 whole, which is shorter than its diff:
```python
import functools

import jax
import jax.numpy as jnp
import numpy as np
from jax import lax
from jax.experimental import pallas as pl
from jax.experimental.pallas import tpu as pltpu
from jax.sharding import PartitionSpec as P

MESH = pl.DeviceIdType.MESH
BF = jnp.bfloat16
F32 = jnp.float32
EPS = 1e-05
MASKED = -1e30
NN = (((1,), (0,)), ((), ()))
NT = (((1,), (1,)), ((), ()))
TN = (((0,), (0,)), ((), ()))
FIRST_RING = 8
LATER_RING = 4


def dot(a, b, dims=NN):
    return lax.dot_general(a, b, dims, preferred_element_type=F32)


def row_loop(total, chunk, body):
    def step(index, carry):
        body(pl.multiple_of(index * chunk, chunk))
        return carry

    lax.fori_loop(0, total // chunk, step, 0)


def tables(width, prior, keys):
    half = width // 2
    frequency = np.exp(-np.log(10000.0) * np.arange(half) / half)
    angles = np.arange(keys)[:, None] * frequency[None, :]
    sine, cosine = np.sin(angles), np.cos(angles)
    features = np.concatenate([cosine, sine], axis=1).astype(np.float32)
    return features, sine[prior:].astype(np.float32), cosine[prior:].astype(np.float32)


def moments(rows):
    average = jnp.mean(rows, axis=-1, keepdims=True)
    centered = rows - average
    spread = jnp.mean(centered * centered, axis=-1, keepdims=True)
    return centered, lax.rsqrt(spread + EPS)


def norm_back(scaled, xhat, inverse):
    along = jnp.mean(scaled * xhat, axis=-1, keepdims=True)
    return (scaled - jnp.mean(scaled, axis=-1, keepdims=True) - xhat * along) * inverse


def gelu_pair(x):
    c = 0.7978845608028654
    square = x * x
    t = jnp.tanh(c * x * (1.0 + 0.044715 * square))
    half = 0.5 * (1.0 + t)
    slope = half + (0.5 * c) * x * (1.0 - t * t) * (1.0 + 0.134145 * square)
    return x * half, slope


def kernel(
    n,
    mem_fill,
    comp_fill,
    gain_attn,
    gain_ffn,
    content_bias,
    position_bias,
    comp_cot,
    segment,
    memory,
    compressed,
    w_qkv,
    w_rel,
    w_out,
    w_up,
    w_down,
    w_comp,
    cotangent,
    features,
    sine,
    cosine,
    layer_out,
    new_rows,
    input_grad,
    gain_attn_out,
    qkv_out,
    cbias_out,
    pbias_out,
    rel_out,
    outp_out,
    gain_ffn_out,
    up_out,
    down_out,
    comp_out,
    seg_v,
    mem_v,
    cmp_v,
    cot_v,
    wqkv,
    wrel,
    wout,
    wup,
    wdn,
    kf,
    qsin,
    qcos,
    vals,
    rot,
    pin,
    normed,
    probs,
    mix,
    mgrad,
    dseg,
    resid,
    rgrad,
    ccot,
    maskrow,
    grads,
    part,
    core_in,
    x_in,
    total,
    small,
    small_in,
    tiny,
    tiny_in,
    first_in,
    later_in,
    in_sem,
    out_sem,
    first_send,
    first_recv,
    first_free,
    later_send,
    later_recv,
    later_free,
    core_send,
    core_recv,
    core_free,
    x_send,
    x_recv,
    x_free,
    back_send,
    back_recv,
    back_free,
    small_send,
    small_recv,
    tiny_send,
    tiny_recv,
):
    steps = n.bit_length() - 1
    width = seg_v.shape[1]
    rows = seg_v.shape[0]
    prior = 2 * rows
    head_size = content_bias.shape[0]
    scale = head_size ** (-0.5)
    piece = width // n
    new_count = comp_cot.shape[0]
    pad_count = ccot.shape[0]

    dp = lax.axis_index("dp")
    head = lax.axis_index("head")
    core = lax.rem(head, 2)
    other = 1 - core
    core_peer = (dp, head + 1 - 2 * core)
    x_peer = (dp, lax.rem(head + 2, 4))
    bits = [lax.rem(dp // (1 << s), 2) for s in range(steps)]
    dp_peers = [(dp + (1 - 2 * bits[s]) * (1 << s), head) for s in range(steps)]

    loads = {}

    def load(name, index, source, target):
        copy = pltpu.make_async_copy(source, target, in_sem.at[index])
        copy.start()
        loads[name] = copy

    def loaded(name):
        loads.pop(name).wait()

    load("memory", 0, memory, mem_v)
    for tap in range(3):
        load(
            f"w_comp{tap}",
            1 + tap,
            w_comp.at[pl.ds(tap * width, width)],
            wup.at[:, pl.ds(256 * tap, 256)],
        )
    load("compressed", 4, compressed, cmp_v)
    load("segment", 5, segment, seg_v)
    load("w_qkv", 6, w_qkv, wqkv)
    load("w_rel", 7, w_rel, wrel)
    load("sine", 8, sine, qsin)
    load("cosine", 9, cosine, qcos)
    load("features", 10, features, kf.at[:, pl.ds(head_size, width)])
    load("w_out", 11, w_out, wout)
    load("cotangent", 12, cotangent, cot_v)
    load("w_down", 13, w_down, wdn)

    barrier = pltpu.get_barrier_semaphore()
    greeted = [core_peer, x_peer] + dp_peers
    for peer in greeted:
        pl.semaphore_signal(barrier, inc=1, device_id=peer, device_id_type=MESH)
    pl.semaphore_wait(barrier, len(greeted))

    def remote(source, target, send, recv, peer):
        copy = pltpu.make_async_remote_copy(
            src_ref=source,
            dst_ref=target,
            send_sem=send,
            recv_sem=recv,
            device_id=peer,
            device_id_type=MESH,
        )
        copy.start()
        return copy

    low_first = list(range(steps))
    low_last = low_first[1:] + [0]
    units = []
    for t in range(3):
        units.append((t, low_first, comp_out.at[pl.ds(t * piece, piece), :]))
    for t in range(4):
        units.append((3 + t, low_first, down_out.at[:, pl.ds(256 * t, 256)]))
    for t in range(4):
        units.append((7 + t, low_first, up_out.at[:, pl.ds(256 * t, 256)]))
    for t in range(3):
        units.append((t, low_first, qkv_out.at[:, pl.ds(256 * t, 256)]))
    units.append((11, low_last, outp_out.at[...]))
    units.append((12, low_last, rel_out.at[...]))
    COMP, DOWN, UP, QKV, OUT, REL = 0, 3, 7, 11, 14, 15
    outs = {}
    sends = {}
    done = set()

    def place(order, j):
        found = 0
        for bit in order:
            found = 2 * found + ((j >> bit) & 1)
        return found

    def store_rows(unit, j, value, lanes=slice(None)):
        at, order, _ = units[unit]
        row = place(order, j) * piece
        grads[2 * at + row // 512, pl.ds(row % 512, piece), lanes] = value

    def store_unit(unit, value, lanes=slice(None)):
        for j in range(n):
            store_rows(unit, j, value[piece * j : piece * (j + 1)], lanes)

    def region(unit, step, mine):
        at, order, _ = units[unit]
        first = bits[order[0]]
        if step == 0:
            return 2 * at + (first if mine else 1 - first), 0, 512
        start = 0
        for s in range(1, step):
            start = start + bits[order[s]] * (width >> (s + 1))
        length = width >> (step + 1)
        mybit = bits[order[step]]
        start = start + (mybit if mine else 1 - mybit) * length
        return 2 * at + first, pl.multiple_of(start, length), length

    def slot_refs(unit, step):
        if step == 0:
            slot = unit % FIRST_RING
            return first_in.at[slot], first_send.at[slot], first_recv.at[slot]
        slot = unit % LATER_RING
        index = (step - 1) * LATER_RING + slot
        length = width >> (step + 1)
        begin = 512 - (512 >> (step - 1))
        return (
            later_in.at[slot, pl.ds(begin, length), :],
            later_send.at[index],
            later_recv.at[index],
        )

    def slot_free(unit, step):
        kind = int(units[unit][1] is low_last)
        if step == 0:
            return first_free.at[kind, unit % FIRST_RING]
        return later_free.at[kind, (step - 1) * LATER_RING + unit % LATER_RING]

    def ring(step):
        return FIRST_RING if step == 0 else LATER_RING

    def unit_send(unit, step):
        target, send, recv = slot_refs(unit, step)
        if unit >= ring(step):
            assert (unit - ring(step), "done") in done
            pl.semaphore_wait(slot_free(unit, step), 1)
        at, start, length = region(unit, step, False)
        peer = dp_peers[units[unit][1][step]]
        sends[unit, step] = remote(grads.at[at, pl.ds(start, length), :], target, send, recv, peer)

    def unit_step(unit, step):
        if unit < 0 or unit >= len(units) or (unit, step) in done:
            return
        done.add((unit, step))
        target = slot_refs(unit, step)[0]
        sends[unit, step].wait_recv()
        at, start, length = region(unit, step, True)
        chunk = min(64, length)

        def add(offset):
            here = pl.ds(pl.multiple_of(start + offset, chunk), chunk)
            grads[at, here, :] = grads[at, here, :] + target[pl.ds(offset, chunk), :]

        row_loop(length, chunk, add)
        later = unit + ring(step)
        if later < len(units):
            peer = dp_peers[units[later][1][step]]
            pl.semaphore_signal(
                slot_free(later, step), inc=1, device_id=peer, device_id_type=MESH
            )
        if step + 1 < steps:
            unit_send(unit, step + 1)
        else:
            for s in range(steps):
                sends.pop((unit, s)).wait_send()
            copy = pltpu.make_async_copy(
                grads.at[at, pl.ds(start, length), :], units[unit][2], out_sem.at[unit]
            )
            copy.start()
            outs[unit] = copy
            done.add((unit, "done"))

    lag = 1 if steps <= LATER_RING - 1 else 0

    def tick(unit):
        for step in range(steps):
            unit_step(unit - step * lag, step)

    def drain(first, last):
        for unit in range(last, last + steps):
            for step in range(1, steps):
                if first <= unit + 1 - step <= last:
                    unit_step(unit + 1 - step, step)

    moves = {}
    subs = 4
    sub_rows = rows // subs

    def span(sub):
        return pl.ds(sub * sub_rows, sub_rows)

    def sum_source(k):
        return (grads, 22) if k == 2 else (part, 0)

    def sum_start(k, sub):
        if k >= 1 and sub == 0:
            pl.semaphore_wait(core_free, 1)
        ref, base = sum_source(k)
        moves[k, "core", sub] = remote(
            ref.at[pl.ds(base + 2 * other, 2), span(sub), :],
            core_in.at[:, span(sub), :],
            core_send.at[sub],
            core_recv.at[sub],
            core_peer,
        )

    def sum_across(k, sub):
        ref, base = sum_source(k)
        moves[k, "core", sub].wait()
        for i in range(2):
            at = base + 2 * core + i
            ref[at, span(sub), :] = ref[at, span(sub), :] + core_in[i, span(sub), :]
        if sub == subs - 1 and k < 3:
            pl.semaphore_signal(core_free, inc=1, device_id=core_peer, device_id_type=MESH)
        if k >= 2 and sub == 0:
            pl.semaphore_wait(x_free.at[k % 2], 1)
        moves[k, "x", sub] = remote(
            ref.at[pl.ds(base + 2 * core, 2), span(sub), :],
            x_in.at[k % 2, :, span(sub), :],
            x_send.at[k % 2, sub],
            x_recv.at[k % 2, sub],
            x_peer,
        )

    def sum_back(k, sub):
        ref, base = sum_source(k)
        moves[k, "x", sub].wait_recv()
        for i in range(2):
            total[2 * core + i, span(sub), :] = (
                ref[base + 2 * core + i, span(sub), :] + x_in[k % 2, i, span(sub), :]
            )
        if sub == subs - 1 and k < 2:
            pl.semaphore_signal(x_free.at[k % 2], inc=1, device_id=x_peer, device_id_type=MESH)
        if k >= 1 and sub == 0:
            pl.semaphore_wait(back_free, 1)
        here = total.at[pl.ds(2 * core, 2), span(sub), :]
        moves[k, "back", sub] = remote(here, here, back_send.at[sub], back_recv.at[sub], core_peer)

    def sum_done(k, sub):
        moves[k, "back", sub].wait_recv()

    def sum_used(k):
        for sub in range(subs):
            moves[k, "x", sub].wait_send()
            moves[k, "back", sub].wait_send()
        if k < 3:
            pl.semaphore_signal(back_free, inc=1, device_id=core_peer, device_id_type=MESH)

    def total_rows(here):
        return jnp.concatenate([total[t, here, :] for t in range(4)], axis=1)

    ccot[...] = jnp.zeros_like(ccot)
    ccot[0:new_count, :] = comp_cot[...]
    loaded("memory")
    fill = mem_fill[0]
    compressed_rows = jnp.zeros((pad_count, 256), F32)
    row_at = lax.broadcasted_iota(jnp.int32, (pad_count, rows), 0)
    slot_at = lax.broadcasted_iota(jnp.int32, (pad_count, rows), 1)
    for tap in range(3):
        pick = (slot_at == 3 * row_at + tap) & (slot_at >= rows - fill) & (row_at < new_count)
        window = dot(jnp.where(pick, 1.0, 0.0).astype(BF), mem_v[...]).astype(BF)
        loaded(f"w_comp{tap}")
        compressed_rows = compressed_rows + dot(window, wup[:, pl.ds(256 * tap, 256)])
        tap_grad = dot(window, ccot[...], TN)
        for i in range(n):
            j, t = divmod(n * tap + i, 3)
            store_rows(COMP + t, j, tap_grad[piece * i : piece * (i + 1)])
    new_rows[...] = compressed_rows[0:new_count].astype(BF)
    for t in range(3):
        unit_send(COMP + t, 0)
    load("w_up", 1, w_up, wup)

    lane = lax.broadcasted_iota(jnp.int32, (1, rows), 1)
    maskrow[0:1, 0:rows] = jnp.where(lane >= rows - comp_fill[0], 0.0, MASKED)
    maskrow[0:1, rows:prior] = jnp.where(lane >= rows - fill, 0.0, MASKED)

    def norm_into(source, base):
        def body(offset):
            centered, inverse = moments(source[pl.ds(offset, 32), :].astype(F32))
            normed[pl.ds(pl.multiple_of(base + offset, 32), 32), :] = (
                centered * inverse * gain_attn[...]
            ).astype(BF)

        row_loop(rows, 32, body)

    loaded("compressed")
    norm_into(cmp_v, 0)
    norm_into(mem_v, rows)
    loaded("segment")
    norm_into(seg_v, prior)

    def bias_row(ref, h):
        line = lax.broadcasted_iota(jnp.int32, (head_size, head_size), 0)
        column = lax.broadcasted_iota(jnp.int32, (head_size, head_size), 1)
        return jnp.sum(jnp.where(line == column, ref[:, h : h + 1], 0.0), axis=0, keepdims=True)

    loaded("w_qkv")
    loaded("features")
    dh = head_size
    key_lane = (0, dh + width)
    pair_lane = (0, dh)
    place_lane = (dh, 0)
    query_lane = (0, width)
    for block in range(2):
        here = pl.ds(block * rows, rows)
        for h in range(2):
            both = dot(normed[here, :], wqkv[:, 3 * dh * h + dh : 3 * dh * (h + 1)])
            kf[here, key_lane[h] : key_lane[h] + dh] = both[:, 0:dh].astype(BF)
            vals[here, dh * h : dh * (h + 1)] = both[:, dh:].astype(BF)
    here = pl.ds(prior, rows)
    queries = [None, None]
    three = [dot(normed[here, :], wqkv[:, 256 * t : 256 * (t + 1)]) for t in range(3)]
    queries[0] = three[0][:, 0:dh]
    kf[here, key_lane[0] : key_lane[0] + dh] = three[0][:, dh:].astype(BF)
    vals[here, 0:dh] = three[1][:, 0:dh].astype(BF)
    queries[1] = three[1][:, dh:]
    kf[here, key_lane[1] : key_lane[1] + dh] = three[2][:, 0:dh].astype(BF)
    vals[here, dh : 2 * dh] = three[2][:, dh:].astype(BF)
    for h in range(2):
        rot[h, :, query_lane[h] : query_lane[h] + dh] = (
            queries[h] + bias_row(content_bias, h)
        ).astype(BF)
        pin[:, dh * h : dh * (h + 1)] = (queries[h] + bias_row(position_bias, h)).astype(BF)

    loaded("w_rel")
    loaded("sine")
    loaded("cosine")
    half = width // 2
    for h in range(2):
        for j in range(2):
            cols = slice(256 * j, 256 * (j + 1))
            weights = wrel[256 * j : 256 * (j + 1), dh * h : dh * (h + 1)]
            upper = dot(pin[:, dh * h : dh * (h + 1)], weights, NT)
            weights = wrel[half + 256 * j : half + 256 * (j + 1), dh * h : dh * (h + 1)]
            lower = dot(pin[:, dh * h : dh * (h + 1)], weights, NT)
            begin = place_lane[h] + 256 * j
            rot[h, :, begin : begin + 256] = (
                upper * qsin[:, cols] + lower * qcos[:, cols]
            ).astype(BF)
            rot[h, :, begin + half : begin + half + 256] = (
                lower * qsin[:, cols] - upper * qcos[:, cols]
            ).astype(BF)

    block_rows = rows // 2
    probs[:, 0:block_rows, prior + 256 : prior + 512] = jnp.zeros((2, block_rows, 256), BF)
    for block in range(2):
        here = pl.ds(block * block_rows, block_rows)
        tiles = 5 + block
        for h in range(2):

            def score_tile(t, carry, h=h, here=here):
                keys = pl.ds(pl.multiple_of(t * 256, 256), 256)
                grads[6 + t, 0:block_rows, :] = dot(
                    rot[h, here, :], kf[keys, pair_lane[h] : pair_lane[h] + dh + width], NT
                )
                return carry

            lax.fori_loop(0, tiles, score_tile, 0)

            def soften(offset, h=h, block=block, tiles=tiles):
                inner = pl.ds(offset, 16)
                pieces = []
                for t in range(tiles):
                    s = grads[6 + t, inner, :] * scale
                    if t < 4:
                        s = s + maskrow[0:1, 256 * t : 256 * (t + 1)]
                    if t == tiles - 1:
                        line = lax.broadcasted_iota(jnp.int32, (16, 256), 0) + offset
                        column = lax.broadcasted_iota(jnp.int32, (16, 256), 1)
                        s = jnp.where(column <= line, s, MASKED)
                    pieces.append(s)
                top = functools.reduce(jnp.maximum, pieces)
                top = jnp.max(top, axis=-1, keepdims=True)
                raised = [jnp.exp(s - top) for s in pieces]
                whole = jnp.sum(functools.reduce(jnp.add, raised), axis=-1, keepdims=True)
                inverse = 1.0 / whole
                outer = pl.ds(pl.multiple_of(block * block_rows + offset, 16), 16)
                for t in range(tiles):
                    probs[h, outer, 256 * t : 256 * (t + 1)] = (raised[t] * inverse).astype(BF)

            row_loop(block_rows, 16, soften)
            mix[here, dh * h : dh * (h + 1)] = dot(
                probs[h, here, 0 : 256 * tiles], vals[0 : 256 * tiles, dh * h : dh * (h + 1)]
            ).astype(BF)
        if block == 0:
            loaded("w_out")
        for t in range(4):
            part[t, here, :] = dot(mix[here, :], wout[256 * t : 256 * (t + 1), :], NT)
        for sub in (2 * block, 2 * block + 1):
            sum_start(0, sub)
        if block == 0:
            tick(COMP)
        for sub in (2 * block, 2 * block + 1):
            sum_across(0, sub)

    loaded("cotangent")
    loaded("w_down")
    for t in range(4):
        cols = pl.ds(256 * t, 256)
        rgrad[:, cols] = dot(cot_v[...], wdn[:, cols])

    nf, act = mem_v, cmp_v
    for sub in range(subs):
        sum_back(0, sub)
        if sub in (1, 3):
            tick(COMP + 1 + sub // 2)
        sum_done(0, sub)

        def residual_rows(offset, sub=sub):
            here = pl.ds(pl.multiple_of(sub * sub_rows + offset, 32), 32)
            value = seg_v[here, :].astype(F32) + total_rows(here)
            resid[here, :] = value
            centered, inverse = moments(value)
            nf[here, :] = (centered * inverse * gain_ffn[...]).astype(BF)

        row_loop(sub_rows, 32, residual_rows)
    sum_used(0)

    loaded("w_up")
    hidden_lane = place_lane[0]
    for t in range(4):
        cols = slice(256 * t, 256 * (t + 1))
        value, slope = gelu_pair(dot(nf[...], wup[:, cols]))
        act[:, cols] = value.astype(BF)
        rot[0, :, hidden_lane + 256 * t : hidden_lane + 256 * (t + 1)] = (
            rgrad[:, cols] * slope
        ).astype(BF)
        store_unit(DOWN + t, dot(cot_v[...], act[:, cols], TN))
        unit_send(DOWN + t, 0)

    def hidden_grad():
        return rot[0, :, hidden_lane : hidden_lane + width]

    for which in (other, core):
        for i in range(2):
            lines = pl.ds(pl.multiple_of(512 * which + 256 * i, 256), 256)
            part[2 * which + i] = dot(hidden_grad(), wup[lines, :], NT)
        if which is other:
            for sub in range(subs):
                sum_start(1, sub)
    for sub in range(subs):
        sum_across(1, sub)
    drain(COMP, COMP + 2)
    for t in range(4):
        cols = slice(hidden_lane + 256 * t, hidden_lane + 256 * (t + 1))
        store_unit(UP + t, dot(nf[...], rot[0, :, cols], TN))
        unit_send(UP + t, 0)
    for t in range(4):
        grads[22 + t] = dot(act[...], wdn[256 * t : 256 * (t + 1), :], NT)
    for sub in range(subs):
        sum_start(2, sub)

    agrad = mem_v
    small[...] = jnp.zeros_like(small)
    for sub in range(subs):
        sum_back(1, sub)
        if sub == 2:
            tick(DOWN)
        sum_done(1, sub)

        def residual_back(offset, carry, sub=sub):
            here = pl.ds(pl.multiple_of(sub * sub_rows + offset * 32, 32), 32)
            grad = total_rows(here)
            centered, inverse = moments(resid[here, :])
            xhat = centered * inverse
            back = norm_back(grad * gain_ffn[...], xhat, inverse)
            value = cot_v[here, :].astype(F32) + back
            rgrad[here, :] = value
            agrad[here, :] = value.astype(BF)
            return carry + jnp.sum(grad * xhat, axis=0, keepdims=True)

        gain_part = lax.fori_loop(
            0, sub_rows // 32, residual_back, jnp.zeros((1, width), F32)
        )
        for j in range(width // 128):
            line = slice(8 + j, 9 + j)
            small[line, :] = small[line, :] + gain_part[:, 128 * j : 128 * (j + 1)]
    sum_used(1)
    for sub in range(subs):
        sum_across(2, sub)
    tick(DOWN + 1)

    mgrad[...] = dot(agrad[...], wout[...]).astype(BF)
    for h in range(2):
        wup[:, 3 * dh * h : 3 * dh * h + dh] = jnp.zeros((prior, dh), BF)
    for h in range(2):
        lanes = slice(dh * h, dh * (h + 1))
        col = 3 * dh * h
        mg = mgrad[:, lanes]
        delta = jnp.sum(mg.astype(F32) * mix[:, lanes].astype(F32), axis=-1, keepdims=True)

        def key_tile(t, target, lines, ds_rows, ds_cols, h=h, lanes=lanes, col=col, mg=mg, delta=delta):
            keys = pl.ds(pl.multiple_of(t * 256, 256), 256)
            p = probs[h, :, keys]
            dp_tile = dot(mg, vals[keys, lanes], NT)
            ds = (p.astype(F32) * (dp_tile - delta)).astype(BF)
            wdn[ds_rows, ds_cols] = ds
            cq = rot[h, :, query_lane[h] : query_lane[h] + dh]
            target[lines, col + dh : col + 2 * dh] = (dot(ds, cq, TN) * scale).astype(BF)
            target[lines, col + 2 * dh : col + 3 * dh] = dot(p, mg, TN).astype(BF)

        def prior_tile(t, carry):
            at = pl.ds(pl.multiple_of(t * 256, 256), 256)
            key_tile(t, wup, at, slice(0, rows), at)
            return carry

        lax.fori_loop(0, 4, prior_tile, 0)
        for t in range(2):
            at = slice(256 * t, 256 * (t + 1))
            key_tile(4 + t, dseg, at, slice(rows, 2 * rows), at)

        def times_keys(cols):
            return (
                dot(wdn[0:rows, :], kf[0:prior, cols])
                + dot(wdn[rows : 2 * rows, 0:rows], kf[prior : prior + rows, cols])
            ) * scale

        for j in range(2):
            cols = slice(256 * j, 256 * (j + 1))
            upper = times_keys(slice(dh + 256 * j, dh + 256 * (j + 1)))
            lower = times_keys(slice(dh + half + 256 * j, dh + half + 256 * (j + 1)))
            begin = place_lane[h] + 256 * j
            rot[h, :, begin : begin + 256] = (
                upper * qsin[:, cols] - lower * qcos[:, cols]
            ).astype(BF)
            rot[h, :, begin + half : begin + half + 256] = (
                upper * qcos[:, cols] + lower * qsin[:, cols]
            ).astype(BF)
        content = times_keys(slice(key_lane[h], key_lane[h] + dh))
        position = dot(rot[h, :, place_lane[h] : place_lane[h] + width], wrel[:, lanes])
        dseg[:, col : col + dh] = (content + position).astype(BF)
        small[h : h + 1, :] = jnp.sum(content, axis=0, keepdims=True)
        small[2 + h : 3 + h, :] = jnp.sum(position, axis=0, keepdims=True)
        if h == 0:
            tick(DOWN + 2)

    stage = cmp_v
    for sub in range(subs):
        sum_back(2, sub)
    tick(DOWN + 3)
    for which in (other, core):
        for i in range(2):
            lines = pl.ds(pl.multiple_of(512 * which + 256 * i, 256), 256)
            part[2 * which + i] = dot(dseg[...], wqkv[lines, :], NT)
        if which is other:
            for sub in range(subs):
                sum_start(3, sub)
    for sub in range(subs):
        sum_across(3, sub)
    for sub in range(subs):
        sum_done(2, sub)

        def output_rows(offset, sub=sub):
            here = pl.ds(pl.multiple_of(sub * sub_rows + offset, 32), 32)
            stage[here, :] = (resid[here, :] + total_rows(here)).astype(BF)

        row_loop(sub_rows, 32, output_rows)
    sum_used(2)
    out_copy = pltpu.make_async_copy(stage, layer_out, out_sem.at[16])
    out_copy.start()

    drain(DOWN, DOWN + 3)
    for t in range(3):
        outs.pop(COMP + t).wait()
        cols = slice(256 * t, 256 * (t + 1))
        store_unit(
            QKV + t,
            dot(normed[0:prior, :], wup[:, cols], TN) + dot(normed[prior:, :], dseg[:, cols], TN),
        )
        unit_send(QKV + t, 0)
    store_unit(OUT, dot(agrad[...], mix[...], TN))
    for h in range(2):
        lanes = slice(dh * h, dh * (h + 1))
        store_unit(
            REL,
            dot(rot[h, :, place_lane[h] : place_lane[h] + width], pin[:, lanes], TN),
            lanes,
        )
    unit_send(OUT, 0)

    for s in range(steps):
        copy = remote(small, small_in.at[s], small_send.at[s], small_recv.at[s], dp_peers[s])
        copy.wait()
        small[...] = small[...] + small_in[s]

    tick(UP)

    for sub in range(subs):
        sum_back(3, sub)
        sum_done(3, sub)

        def input_rows(offset, sub=sub):
            here = pl.ds(pl.multiple_of(sub * sub_rows + offset, 32), 32)
            centered, inverse = moments(seg_v[here, :].astype(F32))
            back = norm_back(total_rows(here) * gain_attn[...], centered * inverse, inverse)
            resid[here, :] = rgrad[here, :] + back

        row_loop(sub_rows, 32, input_rows)
    sum_used(3)
    grad_copy = pltpu.make_async_copy(resid, input_grad, out_sem.at[17])
    grad_copy.start()

    line = lax.broadcasted_iota(jnp.int32, (piece, width), 0)
    column = lax.broadcasted_iota(jnp.int32, (piece, width), 1)
    mine = column == dp * piece + line

    def own_column(row):
        return jnp.sum(jnp.where(mine, row, 0.0), axis=-1, keepdims=True)

    def as_row(values):
        line = lax.broadcasted_iota(jnp.int32, (piece, 128), 0)
        column = lax.broadcasted_iota(jnp.int32, (piece, 128), 1)
        return jnp.sum(jnp.where(line == column, values, 0.0), axis=0, keepdims=True)

    gain_row = jnp.concatenate([small[8 + j : 9 + j, :] for j in range(width // 128)], axis=1)
    gain_ffn_out[...] = as_row(own_column(gain_row))[:, 0:piece]
    bias_piece = head_size // n
    line = lax.broadcasted_iota(jnp.int32, (bias_piece, head_size), 0)
    column = lax.broadcasted_iota(jnp.int32, (bias_piece, head_size), 1)
    owned = column == dp * bias_piece + line
    for h in range(2):
        cbias_out[:, h : h + 1] = jnp.sum(
            jnp.where(owned, small[h : h + 1, :], 0.0), axis=-1, keepdims=True
        )
        pbias_out[:, h : h + 1] = jnp.sum(
            jnp.where(owned, small[2 + h : 3 + h, :], 0.0), axis=-1, keepdims=True
        )

    for unit in range(UP + 1, REL + 1):
        tick(unit)
        if unit == UP + 3:
            unit_send(REL, 0)
    drain(UP, REL)

    own = pl.ds(pl.multiple_of(dp * piece, piece), piece)
    gathered = jnp.zeros((piece, 1), F32)
    for t in range(3):
        at, start, length = region(QKV + t, steps - 1, True)
        product = grads[at, pl.ds(start, length), :] * wqkv[
            own, 256 * t : 256 * (t + 1)
        ].astype(F32)
        gathered = gathered + jnp.sum(product, axis=-1, keepdims=True)
    tiny[0:1, :] = as_row(gathered / own_column(gain_attn[...]))
    for s, peer in enumerate((core_peer, x_peer)):
        copy = remote(tiny, tiny_in.at[s], tiny_send.at[s], tiny_recv.at[s], peer)
        copy.wait()
        tiny[...] = tiny[...] + tiny_in[s]
    gain_attn_out[...] = tiny[0:1, 0:piece]

    for copy in outs.values():
        copy.wait()
    out_copy.wait()
    grad_copy.wait()


def shards(
    n,
    segment,
    memory,
    compressed,
    mem_fill,
    comp_fill,
    gain_attn,
    w_qkv,
    content_bias,
    position_bias,
    w_rel,
    w_out,
    gain_ffn,
    w_up,
    w_down,
    w_comp,
    out_cotangent,
    comp_cotangent,
):
    rows, width = segment.shape[1:]
    keys = 3 * rows
    steps = n.bit_length() - 1
    piece = width // n
    head_size = content_bias.shape[0]
    new_count = comp_cotangent.shape[1]
    pad_count = -(-new_count // 16) * 16
    features, sine, cosine = tables(width, 2 * rows, keys)
    vm, anyw = pl.BlockSpec(memory_space=pltpu.VMEM), pl.BlockSpec(memory_space=pl.ANY)
    smem = pl.BlockSpec(memory_space=pltpu.SMEM)
    dma = pltpu.SemaphoreType.DMA
    plain = pltpu.SemaphoreType.REGULAR
    later_count = LATER_RING * max(steps - 1, 1)
    scratch = [
        pltpu.VMEM((rows, width), BF),
        pltpu.VMEM((rows, width), BF),
        pltpu.VMEM((rows, width), BF),
        pltpu.VMEM((rows, width), BF),
        pltpu.VMEM(w_qkv.shape, BF),
        pltpu.VMEM(w_rel.shape, BF),
        pltpu.VMEM(w_out.shape, BF),
        pltpu.VMEM(w_up.shape, BF),
        pltpu.VMEM(w_down.shape, BF),
        pltpu.VMEM((keys, width + 2 * head_size), BF),
        pltpu.VMEM((rows, width // 2), F32),
        pltpu.VMEM((rows, width // 2), F32),
        pltpu.VMEM((keys, 2 * head_size), BF),
        pltpu.VMEM((2, rows, width + head_size), BF),
        pltpu.VMEM((rows, 2 * head_size), BF),
        pltpu.VMEM((keys, width), BF),
        pltpu.VMEM((2, rows, keys), BF),
        pltpu.VMEM((rows, 2 * head_size), BF),
        pltpu.VMEM((rows, 2 * head_size), BF),
        pltpu.VMEM((rows, 6 * head_size), BF),
        pltpu.VMEM((rows, width), F32),
        pltpu.VMEM((rows, width), F32),
        pltpu.VMEM((pad_count, 256), BF),
        pltpu.VMEM((8, 2 * rows), F32),
        pltpu.VMEM((26, 512, 256), F32),
        pltpu.VMEM((4, rows, 256), F32),
        pltpu.VMEM((2, rows, 256), F32),
        pltpu.VMEM((2, 2, rows, 256), F32),
        pltpu.VMEM((4, rows, 256), F32),
        pltpu.VMEM((16, 128), F32),
        pltpu.VMEM((steps, 16, 128), F32),
        pltpu.VMEM((8, 128), F32),
        pltpu.VMEM((2, 8, 128), F32),
        pltpu.VMEM((FIRST_RING, 512, 256), F32),
        pltpu.VMEM((LATER_RING, 512, 256), F32),
        dma((16,)),
        dma((18,)),
        dma((FIRST_RING,)),
        dma((FIRST_RING,)),
        plain((2, FIRST_RING)),
        dma((later_count,)),
        dma((later_count,)),
        plain((2, later_count)),
        dma((4,)),
        dma((4,)),
        plain,
        dma((2, 4)),
        dma((2, 4)),
        plain((2,)),
        dma((4,)),
        dma((4,)),
        plain,
        dma((steps,)),
        dma((steps,)),
        dma((2,)),
        dma((2,)),
    ]
    shape = jax.ShapeDtypeStruct
    results = pl.pallas_call(
        functools.partial(kernel, n),
        out_shape=(
            shape((rows, width), BF),
            shape((new_count, 256), BF),
            shape((rows, width), F32),
            shape((1, piece), F32),
            shape((piece, w_qkv.shape[1]), F32),
            shape((head_size // n, 2), F32),
            shape((head_size // n, 2), F32),
            shape((piece, w_rel.shape[1]), F32),
            shape((piece, w_out.shape[1]), F32),
            shape((1, piece), F32),
            shape((piece, w_up.shape[1]), F32),
            shape((piece, w_down.shape[1]), F32),
            shape((3 * piece, w_comp.shape[1]), F32),
        ),
        in_specs=[smem] * 2 + [vm] * 5 + [anyw] * 13,
        out_specs=(anyw, vm, anyw, vm, anyw, vm, vm, anyw, anyw, vm, anyw, anyw, anyw),
        scratch_shapes=scratch,
        compiler_params=pltpu.CompilerParams(
            collective_id=0, has_side_effects=True, vmem_limit_bytes=63 * 2**20
        ),
    )(
        mem_fill,
        comp_fill,
        gain_attn.reshape(1, width),
        gain_ffn.reshape(1, width),
        content_bias,
        position_bias,
        comp_cotangent[0],
        segment[0],
        memory[0],
        compressed[0],
        w_qkv,
        w_rel,
        w_out,
        w_up,
        w_down,
        w_comp,
        out_cotangent[0],
        jnp.asarray(features, BF),
        jnp.asarray(sine),
        jnp.asarray(cosine),
    )
    layer, new, grad, gattn, qkv, cbias, pbias, rel, outp, gffn, up, down, comp = results
    return (
        layer[None],
        new[None],
        grad[None],
        gattn.reshape(piece),
        qkv,
        cbias,
        pbias,
        rel,
        outp,
        gffn.reshape(piece),
        up,
        down,
        comp,
    )


def solution(mesh):
    stream = P("dp", None, None)
    split = P(None, "head")
    return jax.shard_map(
        functools.partial(shards, mesh.shape["dp"]),
        mesh=mesh,
        in_specs=(
            stream,
            stream,
            stream,
            P("dp"),
            P("dp"),
            P(),
            split,
            split,
            split,
            split,
            split,
            P(),
            split,
            split,
            split,
            stream,
            P("dp", None, "head"),
        ),
        out_specs=(
            stream,
            P("dp", None, "head"),
            stream,
            P("dp"),
            P("dp", "head"),
            P("dp", "head"),
            P("dp", "head"),
            P("dp", "head"),
            P("dp", "head"),
            P("dp"),
            P("dp", "head"),
            P("dp", "head"),
            P("dp", "head"),
        ),
        check_vma=False,
    )
```

time: 902 us -> 322 us (0.36)
  waiting for transfers between devices: 683 us -> 0 us
  Pallas kernels: 0 us -> 303 us
  matrix products: 78.6 us -> 0 us
  other arithmetic: 53 us -> 0 us
  blocking collectives: 28.3 us -> 0 us
  local copies, waits for them, and re-layouts: 34.2 us -> 16.2 us
  between operations: 17.2 us -> 1.99 us
    reduce_scatter x6 -> x0, waiting for transfers between devices: 438 us -> none  [the longest x1 91.3 us: shards(): lax.psum_scatter(ffn_totals[0], 'dp', scatter_dimension=0, tiled=True)]
    pallas_call x0 -> x1, Pallas kernels: none -> 303 us  [shards(): pl.pallas_call(functools.partial(kernel, n), out_shape=(shape((rows, widt...]
    psum x3 -> x0, waiting for transfers between devices: 184 us -> none  [the longest x1 85.7 us: forward_step(): ffn_out = lax.psum(ffn_part, 'head')]
    dot_general x44 -> x0, matrix products: 78.6 us -> none  [the longest x1 5.36 us: forward_step(): jnp.einsum('sd,sf->df', out_grad, activated, preferred_element_type=jnp.f...]
    unnamed x13 -> x0, waiting for transfers between devices: 60.5 us -> none
    unnamed x1 -> x0, blocking collectives: 22.5 us -> none
    reduce_sum x12 -> x0, other arithmetic: 19.9 us -> none  [the longest x4 6.43 us: norm_rows(): spread = jnp.mean(centered * centered, axis=-1, keepdims=True)]
    another operation x4 -> x0, other arithmetic: 15.3 us -> none
  transfers between devices with their start and end apart: 11 -> 0, of which waited for: 10 -> 0; matrix products, arithmetic and copies ran while one was open for 9% -> 0% of each run, Pallas kernels for 0% -> 0%
where the time goes in v1:
time: 322 us; the launch traced here: 321 us
  Pallas kernels  303 us (94%)
  local copies, waits for them, and re-layouts  16.2 us (5%)
    pallas_call x1, Pallas kernels, shards(): pl.pallas_call(functools.partial(kernel, n), out_shape=(shape((rows, widt...  303 us
    unnamed x33, local copies, waits for them, and re-layouts  16.2 us

profile of v1, /device:TPU:0, one launch (start us, length us, event | category | flops | bytes accessed | tf_op | source)
XLA Modules:
  0.0 321.4 jit_solution(14498609733552096130)
XLA Ops:
  1.9 1.4 copy.33.content_bias
  3.4 1.4 copy.34.position_bias
  4.8 303.2 %shard_map.291 = (bf16[512,1024]{1,0:T(8,128)(2,1)}, bf16[170,256]{1,0:T(8,128)(2,1)}, f32[512,1024]{1,0:T(8,128)}, f32[1,128]{1,0:T(1,128)}, f32[128,768]{1,0:T...) custom-call(s32[1]{0:T(128)S(6)} %copy.48.mem_fill, ...), custom_call_target="tpu_custom_call" | custom-call | tf_op jit(solution)/shard_map/pallas_call | solution.py:908
  307.9 0.0 copy-start
  307.9 1.5 copy.35
  309.4 1.3 copy.36
  310.8 2.3 copy.50
  313.0 1.5 copy.51
  314.6 0.0 copy-done
  314.6 0.0 copy-start.8
  314.6 0.0 copy-start.4
  314.6 0.0 copy-start.6
  314.6 0.0 copy-start.5
  314.6 0.0 copy-start.7
  314.6 0.0 copy-start.2
  314.6 1.3 copy.52
  315.9 0.0 copy-done.8
  315.9 0.5 copy.53
  316.4 0.0 copy-done.4
  316.4 0.7 copy.54
  317.2 0.0 copy-done.6
  317.2 0.7 copy.55
  317.8 0.0 copy-done.5
  317.9 0.7 copy.56
  318.5 0.0 copy-done.7
  318.5 0.5 copy.57
  319.0 0.0 copy-done.2
  319.0 0.8 copy.58
  319.8 0.0 copy-done.1
  319.8 0.8 copy.59
  320.6 0.0 copy-done.3
  320.6 0.7 copy.60
  (2 shorter events, 0.0 us)
Async XLA Ops:
  307.9 6.6 %copy-start = (f32[512,1024]{1,0:T(8,128)S(1)}, f32[512,1024]{1,0:T(8,128)}, u32[]{:S(2)}) copy-start(f32[512,1024]{1,0:T(8,128)} %get-tuple-element.28) | copy-start | bytes 6291460
  314.6 1.4 copy-start.8
  314.6 1.9 copy-start.4
  314.6 2.6 copy-start.6
  314.6 3.3 %copy-start.5 = (f32[128,256]{1,0:T(8,128)S(1)}, f32[128,256]{1,0:T(8,128)}, u32[]{:S(2)}) copy-start(f32[128,256]{1,0:T(8,128)} %get-tuple-element.73) | copy-start | bytes 393220
  314.6 3.9 %copy-start.7 = (f32[1,128]{1,0:T(1,128)S(1)}, f32[1,128]{1,0:T(1,128)}, u32[]{:S(2)}) copy-start(f32[1,128]{1,0:T(1,128)} %get-tuple-element.35) | copy-start | bytes 1540
  314.6 4.4 %copy-start.2 = (f32[128,1024]{1,0:T(8,128)S(1)}, f32[128,1024]{1,0:T(8,128)}, u32[]{:S(2)}) copy-start(f32[128,1024]{1,0:T(8,128)} %get-tuple-element.75) | copy-start | bytes 1572868
  315.9 3.9 %copy-start.1 = (f32[128,1024]{1,0:T(8,128)S(1)}, f32[128,1024]{1,0:T(8,128)}, u32[]{:S(2)}) copy-start(f32[128,1024]{1,0:T(8,128)} %get-tuple-element.76) | copy-start | bytes 1572868
  315.9 4.7 %copy-start.3 = (f32[384,256]{1,0:T(8,128)S(1)}, f32[384,256]{1,0:T(8,128)}, u32[]{:S(2)}) copy-start(f32[384,256]{1,0:T(8,128)} %get-tuple-element.77) | copy-start | bytes 1179652
